TPU v7x, 256 devices: a whole 4x4x8 slice. The times are simulated.
256 devices in a mesh: ctx: 32 (over z, x), head: 8 (over y, core).
Axes of the slice: x: 4, y: 4, z: 8, core: 2. Of those that a mesh axis runs over, the one named last changes fastest.
Arguments:
- queries: bfloat16 [8192, 4096], P('ctx', 'head'), may hold values from -6 to 6
- keys: bfloat16 [8192, 4096], P('ctx', 'head'), may hold values from -6 to 6
- values: bfloat16 [8192, 4096], P('ctx', 'head'), may hold values from -6 to 6
- tan_queries: bfloat16 [8192, 4096], P('ctx', 'head'), may hold values from -6 to 6
- tan_keys: bfloat16 [8192, 4096], P('ctx', 'head'), may hold values from -6 to 6
- tan_values: bfloat16 [8192, 4096], P('ctx', 'head'), may hold values from -6 to 6
- w_out: bfloat16 [4096, 4096], P('head'), may hold values from -0.125 to 0.125
Outputs:
- mixed: bfloat16 [4096, 8192], P('head', 'ctx')
- tangent_mixed: bfloat16 [4096, 8192], P('head', 'ctx')
All inputs are finite; a program needn't handle non-finite values.
Results may differ from a plain program's by a relative error of at most 0.022.
Values may be sent and summed in bfloat16 or wider, within the bound.
No kernel may reach another device: no remote copies, remote signals or barrier semaphores. Data moves between devices by JAX's collectives and lax.ppermute only.
A program may use at most 128 MiB of HBM per device.

v0:
```python
import math

import jax
import jax.numpy as jnp
from jax import lax
from jax.experimental import pallas as pl
from jax.experimental.pallas import tpu as pltpu
from jax.sharding import PartitionSpec as P

HD = 128
NX = 4
NZ = 8
NY = 4
HEADS_HERE = 4
LEAF = 256
MASKED = -1e30
LOG_TWO = math.log(2.0)
SCALE = 1.0 / math.sqrt(HD)
F32 = jnp.float32
BF16 = jnp.bfloat16
VMEM = pl.BlockSpec(memory_space=pltpu.VMEM)
HBM = pl.BlockSpec(memory_space=pltpu.HBM)
PARAMS = pltpu.CompilerParams(vmem_limit_bytes=40 * 1024 * 1024)
LARGE = pltpu.CompilerParams(vmem_limit_bytes=63300000)


def dot(a, b):
    return lax.dot_general(a, b, (((1,), (0,)), ((), ())), preferred_element_type=F32)


def dot_nt(a, b):
    return lax.dot_general(a, b, (((1,), (1,)), ((), ())), preferred_element_type=F32)


def pool_matrix(rows):
    out = lax.broadcasted_iota(jnp.int32, (rows, 2 * rows), 0)
    src = lax.broadcasted_iota(jnp.int32, (rows, 2 * rows), 1)
    return jnp.where((src >> 1) == out, 0.5, 0.0).astype(BF16)


def pool(array):
    return dot(pool_matrix(array.shape[0] // 2), array).astype(BF16)


def attend(qq, kv, offset, mask=None):
    scores = dot_nt(qq[:, :HD], kv[:, HD : 2 * HD]) * SCALE + offset
    slopes = dot_nt(qq, kv[:, : 2 * HD]) * SCALE
    if mask is not None:
        scores = jnp.where(mask, scores, MASKED)
    top = jnp.max(scores, axis=1, keepdims=True)
    probs = jnp.exp(scores - top)
    moved = probs * slopes
    den = jnp.sum(probs, axis=1, keepdims=True)
    curv = jnp.sum(moved, axis=1, keepdims=True)
    both = dot(probs.astype(BF16), kv[:, 2 * HD : 4 * HD])
    acc = dot(moved.astype(BF16), kv[:, 2 * HD : 3 * HD]) + both[:, HD:]
    inv = 1.0 / den
    att = both[:, :HD] * inv
    curv = curv * inv
    tan = acc * inv - att * curv
    return att, tan, curv, top + jnp.log(den)


def merge(one, two):
    att1, tan1, curv1, lse1 = one
    att2, tan2, curv2, lse2 = two
    top = jnp.maximum(lse1, lse2)
    e1 = jnp.exp(lse1 - top)
    e2 = jnp.exp(lse2 - top)
    den = e1 + e2
    inv = 1.0 / den
    w1 = e1 * inv
    w2 = e2 * inv
    att = w1 * att1 + w2 * att2
    tan = w1 * tan1 + w2 * tan2 + (w1 * w2) * ((att1 - att2) * (curv1 - curv2))
    return att, tan, w1 * curv1 + w2 * curv2, top + jnp.log(den)


def wide(stats):
    att, tan, curv, lse = stats
    return att, tan, jnp.broadcast_to(curv, att.shape), jnp.broadcast_to(lse, att.shape)


def double(stats, scratch):
    rows = stats[0].shape[0]
    for num, part in enumerate(stats):
        scratch[num, pl.ds(0, rows, 2), :] = part
        scratch[num, pl.ds(1, rows, 2), :] = part
    return tuple(scratch[num, 0 : 2 * rows, :] for num in range(4))


def here():
    ctx = lax.axis_index("ctx")
    return lax.div(ctx, NX), lax.rem(ctx, NX)


def lift_kernel(q, tq, tk, k, v, tv, t0, t1, t2, t3, landed, level3, sems):
    _, x = here()
    copies = [
        pltpu.make_async_copy(ref, landed.at[num], sems.at[num])
        for num, ref in enumerate((q, tq, tk, k, v, tv))
    ]
    for copy in copies:
        copy.start()
    out = lax.broadcasted_iota(jnp.int32, (32, LEAF), 0)
    src = lax.broadcasted_iota(jnp.int32, (32, LEAF), 1)
    matrix = jnp.where((src >> 3) == out, 0.125, 0.0).astype(BF16)
    for num, copy in enumerate(copies):
        copy.wait()
        level3[num] = dot(matrix, landed[num]).astype(BF16)
        for step, out in enumerate((t0, t1, t2, t3)):
            head = lax.rem(x + step, NX)
            cols = pl.ds(pl.multiple_of(head * HD, HD), HD)
            out[:, num * HD : (num + 1) * HD] = level3[num, :, cols]


def pool_kernel(q, tq, tk, k, v, tv, q1, q2, k1, k2):
    matrix = pool_matrix(128)
    for refs, out in (((q, tq), q1), ((tk, k, v, tv), k1)):
        for num, ref in enumerate(refs):
            rows = dot(matrix, ref[...]).astype(BF16)
            for head in range(HEADS_HERE):
                lanes = (head * len(refs) + num) * HD
                out[:, lanes : lanes + HD] = rows[:, head * HD : (head + 1) * HD]
    q2[...] = pool(q1[...])
    k2[...] = pool(k1[...])


def top_kernel(t0, t1, t2, t3, q3, q4, q5, k3, k4, k5):
    level3 = jnp.concatenate([t0[...], t1[...], t2[...], t3[...]], axis=0)
    level4 = pool(level3)
    level5 = pool(level4)
    for rows, q, k in ((level3, q3, k3), (level4, q4, k4), (level5, q5, k5)):
        q[...] = rows[:, : 2 * HD]
        k[...] = rows[:, 2 * HD :]


def mix_kernel(k3, k4, g4, one, two):
    one[0:128, :] = k3[...]
    one[128:160, :] = g4[...]
    two[0:64, :] = k4[...]
    two[64:96, :] = g4[...]


def leaf_kernel(q, tq, tk, k, v, tv, att_out, tan_out, stat_out):
    row = lax.broadcasted_iota(jnp.int32, (LEAF, LEAF), 0)
    col = lax.broadcasted_iota(jnp.int32, (LEAF, LEAF), 1)
    lane = lax.broadcasted_iota(jnp.int32, (LEAF, HD), 1)
    for head in range(HEADS_HERE):
        cols = slice(head * HD, (head + 1) * HD)
        qq = jnp.concatenate([q[:, cols], tq[:, cols]], axis=1)
        kv = jnp.concatenate([tk[:, cols], k[:, cols], v[:, cols], tv[:, cols]], axis=1)
        att, tan, curv, lse = attend(qq, kv, 0.0, row >= col)
        att_out[head] = att
        tan_out[head] = tan
        stat_out[head] = jnp.where(lane == 0, lse, curv)


def far_kernel(q3, q4, q5, g4, g1, g2, g3, o0, o1, o2, o3, scratch):
    z, _ = here()

    def level(q, keys, number, bit):
        att, tan, curv, lse = wide(attend(q[...], keys, number * LOG_TWO))
        seen = ((z >> bit) & 1) == 1
        return att, tan, curv, jnp.where(seen, lse, MASKED)

    keys5 = jnp.concatenate([g4[...], g1[128:160, :], g2[64:96, :], g3[64:96, :]], axis=0)
    carry = level(q5, keys5, 5, 2)
    keys4 = jnp.concatenate([g2[0:64, :], g3[0:64, :]], axis=0)
    carry = merge(level(q4, keys4, 4, 1), double(carry, scratch))
    carry = merge(level(q3, g1[0:128, :], 3, 0), double(carry, scratch))
    att, tan, curv, lse = carry
    lane = lax.broadcasted_iota(jnp.int32, (128, HD), 1)
    stat = jnp.zeros((128, HD), F32)
    at = 0
    for value in (lse, curv):
        for _ in range(3):
            piece = value.astype(BF16).astype(F32)
            stat = jnp.where(lane == at, piece, stat)
            value = value - piece
            at += 1
    for block, out in enumerate((o0, o3, o2, o1)):
        rows = slice(block * 32, (block + 1) * 32)
        out[:, 0:HD] = att[rows].astype(BF16)
        out[:, HD : 2 * HD] = tan[rows].astype(BF16)
        out[:, 2 * HD : 3 * HD] = stat[rows].astype(BF16)


def home_kernel(
    q1, q2, c1, c2, c3, l_att, l_tan, l_stat, att_out, tan_out, stat_out, scratch
):
    _, x = here()
    lane = lax.broadcasted_iota(jnp.int32, (LEAF, HD), 1)

    def level(queries, keys, number, bit):
        att, tan, curv, lse = wide(attend(queries, keys, number * LOG_TWO))
        seen = ((x >> bit) & 1) == 1
        return att, tan, curv, jnp.where(seen, lse, MASKED)

    for head in range(HEADS_HERE):
        qs = slice(head * 2 * HD, (head + 1) * 2 * HD)
        ks = slice(head * 4 * HD, (head + 1) * 4 * HD)
        keys2 = jnp.concatenate([c2[:, ks], c3[:, ks]], axis=0)
        carry = double(level(q2[:, qs], keys2, 2, 1), scratch)
        carry = double(merge(level(q1[:, qs], c1[:, ks], 1, 0), carry), scratch)
        mine = l_stat[head]
        leaf = wide((l_att[head], l_tan[head], mine[:, 1:2], mine[:, 0:1]))
        att, tan, curv, lse = merge(leaf, carry)
        att_out[head] = att
        tan_out[head] = tan
        stat_out[head] = jnp.where(lane == 0, lse, curv)


def finish_kernel(b0, b1, b2, b3, l_att, l_tan, l_stat, out, scratch):
    _, x = here()
    for step, ref in enumerate((b0, b1, b2, b3)):
        head = lax.rem(x + NX - step, NX)
        stat = ref[:, 2 * HD : 3 * HD].astype(F32)
        lse = stat[:, 0:1] + stat[:, 1:2] + stat[:, 2:3]
        curv = stat[:, 3:4] + stat[:, 4:5] + stat[:, 5:6]
        rest = wide((ref[:, 0:HD].astype(F32), ref[:, HD : 2 * HD].astype(F32), curv, lse))
        for _ in range(3):
            rest = double(rest, scratch)
        mine = l_stat[head]
        leaf = wide((l_att[head], l_tan[head], mine[:, 1:2], mine[:, 0:1]))
        att, tan, _, _ = merge(leaf, rest)
        cols = pl.ds(pl.multiple_of(head * HD, HD), HD)
        out[0:LEAF, cols] = att.astype(BF16)
        out[LEAF : 2 * LEAF, cols] = tan.astype(BF16)


def weight_kernel(w, mine, other, landed, sems):
    head = lax.axis_index("head")
    y, core = lax.div(head, 2), lax.rem(head, 2)

    def block(step, flip):
        at = lax.rem(y + step, NY) * 2 + (1 - core if flip else core)
        return w.at[:, pl.ds(pl.multiple_of(at * 512, 512), 512)]

    work = [(step, flip) for flip in (1, 0) for step in range(NY)]
    copies = [
        pltpu.make_async_copy(block(step, flip), landed.at[num], sems.at[num])
        for num, (step, flip) in enumerate(work)
    ]
    for copy in copies:
        copy.start()
    for num, (step, flip) in enumerate(work):
        copies[num].wait()
        (other if flip else mine)[step] = landed[num].T


def project(w1, w2, a1, a2):
    return dot_nt(w1, a1[...]) + dot_nt(w2, a2[...])


def far_chunk_kernel(w1, w2, a1, a2, half_a, half_b):
    both = project(w1[0], w2[0], a1, a2).astype(BF16)
    half_a[...] = both[:256]
    half_b[...] = both[256:]


def near_chunk_kernel(u1, u2, d1, d2, a1, a2, up_b, down_a):
    up_b[...] = project(u1[0, 256:], u2[0, 256:], a1, a2).astype(BF16)
    down_a[...] = project(d1[0, :256], d2[0, :256], a1, a2).astype(BF16)


def own_chunk_kernel(u1, u2, d1, d2, m1, m2, a1, a2, up_a, down_b, own):
    up_a[...] = project(u1[0, :256], u2[0, :256], a1, a2)
    down_b[...] = project(d1[0, 256:], d2[0, 256:], a1, a2)
    own[...] = project(m1[0], m2[0], a1, a2)


def relay_kernel(up_a, got_a, down_b, got_b, send_up, send_down):
    send_up[...] = (up_a[...] + got_a[...].astype(F32)).astype(BF16)
    send_down[...] = (down_b[...] + got_b[...].astype(F32)).astype(BF16)


def total_kernel(own, from_down_a, from_up_a, from_down_b, from_up_b, out, out_tan):
    top = own[:256] + from_down_a[...].astype(F32) + from_up_a[...].astype(F32)
    low = own[256:] + from_down_b[...].astype(F32) + from_up_b[...].astype(F32)
    out[0:256] = top[:, :256].astype(BF16)
    out[256:] = low[:, :256].astype(BF16)
    out_tan[0:256] = top[:, 256:].astype(BF16)
    out_tan[256:] = low[:, 256:].astype(BF16)


def shape(dims, kind=BF16):
    return jax.ShapeDtypeStruct(dims, kind)


def call(kernel, outs, specs, name, flops, size, scratch=(), out_specs=None, grid=(), params=PARAMS):
    return pl.pallas_call(
        kernel,
        out_shape=outs,
        in_specs=specs,
        out_specs=jax.tree.map(lambda _: VMEM, outs) if out_specs is None else out_specs,
        scratch_shapes=list(scratch),
        grid=grid,
        compiler_params=params,
        cost_estimate=pl.CostEstimate(flops=flops, bytes_accessed=size, transcendentals=0),
        name=name,
    )


def x_route(step):
    return [(z * NX + x, z * NX + (x + step) % NX) for z in range(NZ) for x in range(NX)]


def x_to(targets):
    return [(z * NX + x, z * NX + targets[x]) for z in range(NZ) for x in range(NX)]


def z_route(flip):
    return [(z * NX + x, (z ^ flip) * NX + x) for z in range(NZ) for x in range(NX)]


def y_route(step):
    return [(y * 2 + c, ((y + step) % NY) * 2 + c) for y in range(NY) for c in range(2)]


def core_route():
    return [(i, i ^ 1) for i in range(2 * NY)]


def after(first, *rest):
    return lax.optimization_barrier((first,) + rest)


def on_device(queries, keys, values, tan_queries, tan_keys, tan_values, w_out):
    packed_in = (queries, tan_queries, tan_keys, keys, values, tan_values)

    level3 = shape((32, 6 * HD))
    t0, t1, t2, t3 = call(
        lift_kernel,
        (level3,) * 4,
        [HBM] * 6,
        "lift",
        10**9,
        2 * 2**20,
        scratch=[
            pltpu.VMEM((6, LEAF, 4 * HD), BF16),
            pltpu.VMEM((6, 32, 4 * HD), BF16),
            pltpu.SemaphoreType.DMA((6,)),
        ],
        params=LARGE,
    )(*packed_in)
    o_lift = t1
    _, *pool_in = after(t1, *packed_in)
    q1, q2, k1, k2 = call(
        pool_kernel,
        (
            shape((128, 8 * HD)),
            shape((64, 8 * HD)),
            shape((128, 16 * HD)),
            shape((64, 16 * HD)),
        ),
        [VMEM] * 6,
        "pool",
        10**9,
        3 * 2**20,
    )(*pool_in)
    t1 = lax.ppermute(t1, "ctx", x_route(1))
    t3 = lax.ppermute(t3, "ctx", x_route(3))
    t2 = lax.ppermute(t2, "ctx", x_route(2))

    _, *leaf_in = after(o_lift, *packed_in)
    leaf = call(
        leaf_kernel,
        (shape((4, LEAF, HD), F32),) * 3,
        [VMEM] * 6,
        "leaf",
        2 * 10**9,
        5 * 2**20,
    )(*leaf_in)
    t0, *leaf = after(t0, *leaf)
    _, w_later = after(o_lift, w_out)
    w_mine, w_other = call(
        weight_kernel,
        (shape((NY, 512, 512)),) * 2,
        [HBM],
        "weights",
        10**6,
        12 * 2**20,
        scratch=[pltpu.VMEM((2 * NY, 512, 512), BF16), pltpu.SemaphoreType.DMA((2 * NY,))],
    )(w_later)
    t0, w_other = after(t0, w_other)

    t0, q1 = after(t0, q1)
    q3, q4, q5, k3, k4, k5 = call(
        top_kernel,
        tuple(shape((rows, lanes * HD)) for lanes in (2, 4) for rows in (128, 64, 32)),
        [VMEM] * 4,
        "top",
        10**8,
        2**20,
    )(t0, t1, t2, t3)

    g4 = lax.ppermute(k5, "ctx", z_route(7))

    _, k1, k2 = after(k5, k1, k2)
    c1 = lax.ppermute(k1, "ctx", x_to((1, 0, 3, 2)))
    c2 = lax.ppermute(k2, "ctx", x_to((2, 3, 1, 0)))
    c3 = lax.ppermute(k2, "ctx", x_to((3, 2, 1, 0)))

    one, two = call(
        mix_kernel,
        (shape((160, 4 * HD)), shape((96, 4 * HD))),
        [VMEM] * 3,
        "mix",
        10**6,
        2**19,
    )(k3, k4, g4)
    g2 = lax.ppermute(two, "ctx", z_route(2))
    g3 = lax.ppermute(two, "ctx", z_route(3))
    g1 = lax.ppermute(one, "ctx", z_route(1))

    q3, c1, c2, c3 = after(q3, c1, c2, c3)
    back = shape((32, 3 * HD))
    s0, s1, s2, s3 = call(
        far_kernel,
        (back,) * 4,
        [VMEM] * 7,
        "far",
        10**9,
        4 * 2**20,
        scratch=[pltpu.VMEM((4, 128, HD), F32)],
    )(q3, q4, q5, g4, g1, g2, g3)
    _, w_other = after(s1, w_other)
    w_pair = lax.ppermute(w_other, "head", core_route())
    b1 = lax.ppermute(s1, "ctx", x_route(1))
    b3 = lax.ppermute(s3, "ctx", x_route(3))
    b2 = lax.ppermute(s2, "ctx", x_route(2))

    _, q1, *leaf = after(s1, q1, *leaf)
    leaf = call(
        home_kernel,
        (shape((4, LEAF, HD), F32),) * 3,
        [VMEM] * 8,
        "home",
        2 * 10**9,
        4 * 2**20,
        scratch=[pltpu.VMEM((4, 256, HD), F32)],
    )(q1, q2, c1, c2, c3, *leaf)

    rows = 2 * LEAF
    mine = call(
        finish_kernel,
        shape((rows, 4 * HD)),
        [VMEM] * 7,
        "finish",
        10**8,
        3 * 2**20,
        scratch=[pltpu.VMEM((4, 256, HD), F32)],
    )(s0, b1, b2, b3, *leaf)
    pair = lax.ppermute(mine, "head", core_route())

    def chunk(j):
        return pl.BlockSpec((1, 512, 512), lambda i, j=j: (j, 0, 0))

    whole = pl.BlockSpec((rows, 4 * HD), lambda i: (0, 0))
    half = pl.BlockSpec((256, rows), lambda i: (0, 0))
    full = pl.BlockSpec((512, rows), lambda i: (0, 0))
    far_a, far_b = call(
        far_chunk_kernel,
        (shape((256, rows)),) * 2,
        [chunk(2)] * 2 + [whole] * 2,
        "chunk_far",
        5 * 10**8,
        2 * 2**20,
        out_specs=(half,) * 2,
        grid=(1,),
    )(w_mine, w_pair, mine, pair)
    got_a = lax.ppermute(far_a, "head", y_route(1))
    got_b = lax.ppermute(far_b, "head", y_route(3))
    _, mine2, pair2 = after(far_a, mine, pair)
    up_b, down_a = call(
        near_chunk_kernel,
        (shape((256, rows)),) * 2,
        [chunk(1)] * 2 + [chunk(3)] * 2 + [whole] * 2,
        "chunk_near",
        5 * 10**8,
        3 * 2**20,
        out_specs=(half,) * 2,
        grid=(1,),
    )(w_mine, w_pair, w_mine, w_pair, mine2, pair2)
    from_down_b = lax.ppermute(up_b, "head", y_route(1))
    from_up_a = lax.ppermute(down_a, "head", y_route(3))
    _, mine3, pair3 = after(up_b, mine, pair)
    up_a, down_b, own = call(
        own_chunk_kernel,
        (shape((256, rows), F32),) * 2 + (shape((512, rows), F32),),
        [chunk(1)] * 2 + [chunk(3)] * 2 + [chunk(0)] * 2 + [whole] * 2,
        "chunk_own",
        10**9,
        5 * 2**20,
        out_specs=(half, half, full),
        grid=(1,),
    )(w_mine, w_pair, w_mine, w_pair, w_mine, w_pair, mine3, pair3)
    send_up, send_down = call(
        relay_kernel, (shape((256, rows)),) * 2, [VMEM] * 4, "relay", 10**6, 2 * 2**20
    )(up_a, got_a, down_b, got_b)
    from_down_a = lax.ppermute(send_up, "head", y_route(1))
    from_up_b = lax.ppermute(send_down, "head", y_route(3))
    return call(
        total_kernel,
        (shape((512, LEAF)),) * 2,
        [VMEM] * 5,
        "total",
        10**6,
        3 * 2**20,
    )(own, from_down_a, from_up_a, from_down_b, from_up_b)


def solution(mesh):
    return jax.shard_map(
        on_device,
        mesh=mesh,
        in_specs=(P("ctx", "head"),) * 6 + (P("head", None),),
        out_specs=(P("head", "ctx"), P("head", "ctx")),
        check_vma=False,
    )
```

profile of v0, /device:TPU:1, one launch (start us, length us, event | category | flops | bytes accessed | tf_op | source)
XLA Modules:
  0.0 72.9 jit_solution(13216919558373873064)
XLA Ops:
  0.7 2.8 %lift.1 = (bf16[32,768]{1,0:T(8,128)(2,1)}, bf16[32,768]{1,0:T(8,128)(2,1)}, bf16[32,768]{1,0:T(8,128)(2,1)}, bf16[32,768]{1,0:T(8,128)(2,1)}) custom-call(bf16[256,512]{1,0:T(8,128)(2,1)} %q.3, bf16[256,512]{1,0:T(8,128)(2,1)} %tq.3, bf16[256,512]{1,0:T(8,128)(2,1)} %tk.3, bf16[256,512]{1,0:T(8,128)(2,1)} %k.3, bf16[256,512]{1,0:T(8,128)(2,1)} %v.3, ...), custom_call_target="tpu_custom_call" | custom-call | flops 1000000000 | bytes 2097152 | tf_op jit(solution)/shard_map/lift/pallas_call | solution.py:333
  3.5 3.7 %collective-permute-start.1 = (bf16[32,768]{1,0:T(8,128)(2,1)}, bf16[32,768]{1,0:T(8,128)(2,1)S(1)}, u32[]{:S(2)}, u32[]{:S(2)}) collective-permute-start(bf16[32,768]{1,0:T(8,128)(2,1)} %get-tuple-element.87), channel_id=1, source_target_pairs={{0,16},{8,24},{16,0},{24,8},{32,48},{40,56},{48,32},{56,40},{64,80... | collective-permute-start | bytes 147464 | tf_op jit(solution)/shard_map/ppermute | solution.py:364
  8.7 1.4 %leaf.1 = (f32[4,256,128]{2,1,0:T(8,128)S(1)}, f32[4,256,128]{2,1,0:T(8,128)S(1)}, f32[4,256,128]{2,1,0:T(8,128)S(1)}) custom-call(bf16[256,512]{1,0:T(8,128)(2,1)S(1)} %copy-done.1, bf16[256,512]{1,0:T(8,128)(2,1)S(1)} %copy-done.2, bf16[256,512]{1,0:T(8,128)(2,1)S(1)} %copy-done.3, bf16[256,512]{1,0:T(8,128)(2,1)S(1)} %copy-done.4, ...), custom_call_target="tpu_custom_call" | custom-call | flops 2000000000 | bytes 5242880 | tf_op jit(solution)/shard_map/leaf/pallas_call | solution.py:367
  10.2 2.2 %weights.1 = (bf16[4,512,512]{2,1,0:T(8,128)(2,1)S(1)}, bf16[4,512,512]{2,1,0:T(8,128)(2,1)S(1)}) custom-call(bf16[512,4096]{1,0:T(8,128)(2,1)S(1)} %copy-done), custom_call_target="tpu_custom_call" | custom-call | flops 1000000 | bytes 12582912 | tf_op jit(solution)/shard_map/weights/pallas_call | solution.py:377
  14.2 1.5 %collective-permute-start.5 = (bf16[64,2048]{1,0:T(8,128)(2,1)S(1)}, bf16[64,2048]{1,0:T(8,128)(2,1)S(1)}, u32[]{:S(2)}, u32[]{:S(2)}) collective-permute-start(bf16[64,2048]{1,0:T(8,128)(2,1)S(1)} %get-tuple-element.94), channel_id=1, source_target_pairs={{0,24},{8,16},{16,8},{24,0},{32,56},{40,48},{48,40},{56,32},{64,88... | collective-permute-start | bytes 786440 | tf_op jit(solution)/shard_map/ppermute | solution.py:403
  16.9 5.6 %collective-permute-start.6 = (bf16[32,512]{1,0:T(8,128)(2,1)S(1)}, bf16[32,512]{1,0:T(8,128)(2,1)S(1)}, u32[]{:S(2)}, u32[]{:S(2)}) collective-permute-start(bf16[32,512]{1,0:T(8,128)(2,1)S(1)} %get-tuple-element.90), channel_id=1, source_target_pairs={{0,224},{8,232},{16,240},{24,248},{32,192},{40,200},{48,208},{56,2... | collective-permute-start | bytes 98312 | tf_op jit(solution)/shard_map/ppermute | solution.py:398
  22.5 1.6 %collective-permute-done.6.g4 = bf16[32,512]{1,0:T(8,128)(2,1)S(1)} collective-permute-done((bf16[32,512]{1,0:T(8,128)(2,1)S(1)}, bf16[32,512]{1,0:T(8,128)(2,1)S(1)}, u32[]{:S(2)}, u32[]{:S(2)}) %collective-permute-start.6) | collective-permute-done | bytes 32800 | tf_op jit(solution)/shard_map/ppermute | solution.py:398
  24.1 1.4 %collective-permute-start.7 = (bf16[160,512]{1,0:T(8,128)(2,1)S(1)}, bf16[160,512]{1,0:T(8,128)(2,1)S(1)}, u32[]{:S(2)}, u32[]{:S(2)}) collective-permute-start(bf16[160,512]{1,0:T(8,128)(2,1)S(1)} %get-tuple-element.100), channel_id=1, source_target_pairs={{0,32},{8,40},{16,48},{24,56},{32,0},{40,8},{48,16},{56,24},{64,96... | collective-permute-start | bytes 491528 | tf_op jit(solution)/shard_map/ppermute | solution.py:415
  25.5 1.6 %collective-permute-start.9 = (bf16[96,512]{1,0:T(8,128)(2,1)S(1)}, bf16[96,512]{1,0:T(8,128)(2,1)S(1)}, u32[]{:S(2)}, u32[]{:S(2)}) collective-permute-start(bf16[96,512]{1,0:T(8,128)(2,1)S(1)} %get-tuple-element.101), channel_id=1, source_target_pairs={{0,96},{8,104},{16,112},{24,120},{32,64},{40,72},{48,80},{56,88},{... | collective-permute-start | bytes 294920 | tf_op jit(solution)/shard_map/ppermute | solution.py:414
  27.1 2.7 %collective-permute-done.4.c2 = bf16[64,2048]{1,0:T(8,128)(2,1)S(1)} collective-permute-done((bf16[64,2048]{1,0:T(8,128)(2,1)S(1)}, bf16[64,2048]{1,0:T(8,128)(2,1)S(1)}, u32[]{:S(2)}, u32[]{:S(2)}) %collective-permute-start.4) | collective-permute-done | bytes 262176 | tf_op jit(solution)/shard_map/ppermute | solution.py:402
  29.8 1.3 %collective-permute-done.9.g3 = bf16[96,512]{1,0:T(8,128)(2,1)S(1)} collective-permute-done((bf16[96,512]{1,0:T(8,128)(2,1)S(1)}, bf16[96,512]{1,0:T(8,128)(2,1)S(1)}, u32[]{:S(2)}, u32[]{:S(2)}) %collective-permute-start.9) | collective-permute-done | bytes 98336 | tf_op jit(solution)/shard_map/ppermute | solution.py:414
  31.1 5.0 %collective-permute-done.8.g2 = bf16[96,512]{1,0:T(8,128)(2,1)S(1)} collective-permute-done((bf16[96,512]{1,0:T(8,128)(2,1)S(1)}, bf16[96,512]{1,0:T(8,128)(2,1)S(1)}, u32[]{:S(2)}, u32[]{:S(2)}) %collective-permute-start.8) | collective-permute-done | bytes 98336 | tf_op jit(solution)/shard_map/ppermute | solution.py:413
  37.1 1.9 %collective-permute-start.10 = (bf16[4,512,512]{2,1,0:T(8,128)(2,1)S(1)}, bf16[4,512,512]{2,1,0:T(8,128)(2,1)S(1)}, u32[]{:S(2)}, u32[]{:S(2)}) collective-permute-start(bf16[4,512,512]{2,1,0:T(8,128)(2,1)S(1)} %get-tuple-element.104), channel_id=1, source_target_pairs={{0,1},{1,0},{2,3},{3,2},{4,5},{5,4},{6,7},{7,6},{8,9},{9,8},{10,11... | collective-permute-start | bytes 6291464 | tf_op jit(solution)/shard_map/ppermute | solution.py:429
  39.6 2.0 %collective-permute-start.12 = (bf16[32,384]{1,0:T(8,128)(2,1)S(1)}, bf16[32,384]{1,0:T(8,128)(2,1)S(1)}, u32[]{:S(2)}, u32[]{:S(2)}) collective-permute-start(bf16[32,384]{1,0:T(8,128)(2,1)S(1)} %get-tuple-element.106), channel_id=1, source_target_pairs={{0,16},{8,24},{16,0},{24,8},{32,48},{40,56},{48,32},{56,40},{64,80... | collective-permute-start | bytes 73736 | tf_op jit(solution)/shard_map/ppermute | solution.py:432
  42.5 2.2 %home.1 = (f32[4,256,128]{2,1,0:T(8,128)S(1)}, f32[4,256,128]{2,1,0:T(8,128)S(1)}, f32[4,256,128]{2,1,0:T(8,128)S(1)}) custom-call(bf16[128,1024]{1,0:T(8,128)(2,1)S(1)} %get-tuple-element.112.q1, bf16[64,1024]{1,0:T(8,128)(2,1)S(1)} %get-tuple-element.113.q2, bf16[128,2048]{1,0:T(8,128)(2,1)S(1)} %collective-permute-done.3.c1, ...), custom_call_target="tpu_custom_call" | custom-call | flops 2000000000 | bytes 4194304 | tf_op jit(solution)/shard_map/home/pallas_call | solution.py:435
  46.0 1.3 %collective-permute-start.14 = (bf16[512,512]{1,0:T(8,128)(2,1)S(1)}, bf16[512,512]{1,0:T(8,128)(2,1)S(1)}, u32[]{:S(2)}, u32[]{:S(2)}) collective-permute-start(bf16[512,512]{1,0:T(8,128)(2,1)S(1)} %finish.1.a1), channel_id=1, source_target_pairs={{0,1},{1,0},{2,3},{3,2},{4,5},{5,4},{6,7},{7,6},{8,9},{9,8},{10,11... | collective-permute-start | bytes 1572872 | tf_op jit(solution)/shard_map/ppermute | solution.py:455
  47.3 1.5 %collective-permute-done.14.a2 = bf16[512,512]{1,0:T(8,128)(2,1)S(1)} collective-permute-done((bf16[512,512]{1,0:T(8,128)(2,1)S(1)}, bf16[512,512]{1,0:T(8,128)(2,1)S(1)}, u32[]{:S(2)}, u32[]{:S(2)}) %collective-permute-start.14) | collective-permute-done | bytes 524320 | tf_op jit(solution)/shard_map/ppermute | solution.py:455
  49.6 2.8 %collective-permute-start.16 = (bf16[256,512]{1,0:T(8,128)(2,1)S(1)}, bf16[256,512]{1,0:T(8,128)(2,1)S(1)}, u32[]{:S(2)}, u32[]{:S(2)}) collective-permute-start(bf16[256,512]{1,0:T(8,128)(2,1)S(1)} %get-tuple-element.132), channel_id=1, source_target_pairs={{0,6},{1,7},{2,0},{3,1},{4,2},{5,3},{6,4},{7,5},{8,14},{9,15},{10,... | collective-permute-start | bytes 786440 | tf_op jit(solution)/shard_map/ppermute | solution.py:474
  53.3 2.7 %collective-permute-start.18 = (bf16[256,512]{1,0:T(8,128)(2,1)S(1)}, bf16[256,512]{1,0:T(8,128)(2,1)S(1)}, u32[]{:S(2)}, u32[]{:S(2)}) collective-permute-start(bf16[256,512]{1,0:T(8,128)(2,1)S(1)} %get-tuple-element.134), channel_id=1, source_target_pairs={{0,6},{1,7},{2,0},{3,1},{4,2},{5,3},{6,4},{7,5},{8,14},{9,15},{10,... | collective-permute-start | bytes 786440 | tf_op jit(solution)/shard_map/ppermute | solution.py:487
  56.0 1.3 %chunk_own.1 = (f32[256,512]{1,0:T(8,128)S(1)}, f32[256,512]{1,0:T(8,128)S(1)}, f32[512,512]{1,0:T(8,128)S(1)}) custom-call(bf16[4,512,512]{2,1,0:T(8,128)(2,1)S(1)} %get-tuple-element.71.w1.u1.d1.m1, bf16[4,512,512]{2,1,0:T(8,128)(2,1)S(1)} %collective-permute-done.10.w2.u2.d2.m2, bf16[4,512,512]{2,1,0:T(8,128)(2,1)S(1)} %get-tuple-element.71.w1.u1.d1.m1, ...), custom_call_target="tpu_custom_call" | custom-call | flops 1000000000 | bytes 5242880 | tf_op jit(solution)/shard_map/chunk_own/pallas_call | solution.py:489
  57.7 3.1 %collective-permute-done.15.got_a = bf16[256,512]{1,0:T(8,128)(2,1)S(1)} collective-permute-done((bf16[256,512]{1,0:T(8,128)(2,1)S(1)}, bf16[256,512]{1,0:T(8,128)(2,1)S(1)}, u32[]{:S(2)}, u32[]{:S(2)}) %collective-permute-start.15) | collective-permute-done | bytes 262176 | tf_op jit(solution)/shard_map/ppermute | solution.py:473
  61.0 2.7 %collective-permute-start.20 = (bf16[256,512]{1,0:T(8,128)(2,1)S(1)}, bf16[256,512]{1,0:T(8,128)(2,1)S(1)}, u32[]{:S(2)}, u32[]{:S(2)}) collective-permute-start(bf16[256,512]{1,0:T(8,128)(2,1)S(1)} %get-tuple-element.135), channel_id=1, source_target_pairs={{0,6},{1,7},{2,0},{3,1},{4,2},{5,3},{6,4},{7,5},{8,14},{9,15},{10,... | collective-permute-start | bytes 786440 | tf_op jit(solution)/shard_map/ppermute | solution.py:503
  63.7 2.8 %collective-permute-done.19.from_down_b = bf16[256,512]{1,0:T(8,128)(2,1)S(1)} collective-permute-done((bf16[256,512]{1,0:T(8,128)(2,1)S(1)}, bf16[256,512]{1,0:T(8,128)(2,1)S(1)}, u32[]{:S(2)}, u32[]{:S(2)}) %collective-permute-start.19) | collective-permute-done | bytes 262176 | tf_op jit(solution)/shard_map/ppermute | solution.py:486
  66.4 5.6 %collective-permute-done.17.from_down_a = bf16[256,512]{1,0:T(8,128)(2,1)S(1)} collective-permute-done((bf16[256,512]{1,0:T(8,128)(2,1)S(1)}, bf16[256,512]{1,0:T(8,128)(2,1)S(1)}, u32[]{:S(2)}, u32[]{:S(2)}) %collective-permute-start.17) | collective-permute-done | bytes 262176 | tf_op jit(solution)/shard_map/ppermute | solution.py:502
  (48 shorter events, 11.4 us)
Async XLA Ops:
  0.6 8.0 %copy-start.6 = (bf16[256,512]{1,0:T(8,128)(2,1)S(1)}, bf16[256,512]{1,0:T(8,128)(2,1)}, u32[]{:S(2)}) copy-start(bf16[256,512]{1,0:T(8,128)(2,1)} %tv.3) | copy-start | bytes 786436
  0.6 8.0 %copy-start.3 = (bf16[256,512]{1,0:T(8,128)(2,1)S(1)}, bf16[256,512]{1,0:T(8,128)(2,1)}, u32[]{:S(2)}) copy-start(bf16[256,512]{1,0:T(8,128)(2,1)} %tk.3) | copy-start | bytes 786436
  0.7 8.0 %copy-start.2 = (bf16[256,512]{1,0:T(8,128)(2,1)S(1)}, bf16[256,512]{1,0:T(8,128)(2,1)}, u32[]{:S(2)}) copy-start(bf16[256,512]{1,0:T(8,128)(2,1)} %tq.3) | copy-start | bytes 786436
  3.5 9.6 %collective-permute-start.1 = (bf16[32,768]{1,0:T(8,128)(2,1)}, bf16[32,768]{1,0:T(8,128)(2,1)S(1)}, u32[]{:S(2)}, u32[]{:S(2)}) collective-permute-start(bf16[32,768]{1,0:T(8,128)(2,1)} %get-tuple-element.87), channel_id=1, source_target_pairs={{0,16},{8,24},{16,0},{24,8},{32,48},{40,56},{48,32},{56,40},{64,80... | collective-permute-start | bytes 147464 | tf_op jit(solution)/shard_map/ppermute | solution.py:364
  7.1 5.9 %collective-permute-start.2 = (bf16[32,768]{1,0:T(8,128)(2,1)}, bf16[32,768]{1,0:T(8,128)(2,1)S(1)}, u32[]{:S(2)}, u32[]{:S(2)}) collective-permute-start(bf16[32,768]{1,0:T(8,128)(2,1)} %get-tuple-element.88), channel_id=1, source_target_pairs={{0,24},{8,0},{16,8},{24,16},{32,56},{40,32},{48,40},{56,48},{64,88... | collective-permute-start | bytes 147464 | tf_op jit(solution)/shard_map/ppermute | solution.py:363
  8.0 5.1 %collective-permute-start = (bf16[32,768]{1,0:T(8,128)(2,1)}, bf16[32,768]{1,0:T(8,128)(2,1)S(1)}, u32[]{:S(2)}, u32[]{:S(2)}) collective-permute-start(bf16[32,768]{1,0:T(8,128)(2,1)} %get-tuple-element.69), channel_id=1, source_target_pairs={{0,8},{8,16},{16,24},{24,0},{32,40},{40,48},{48,56},{56,32},{64,72... | collective-permute-start | bytes 147464 | tf_op jit(solution)/shard_map/ppermute | solution.py:362
  13.5 16.3 %collective-permute-start.3 = (bf16[128,2048]{1,0:T(8,128)(2,1)S(1)}, bf16[128,2048]{1,0:T(8,128)(2,1)S(1)}, u32[]{:S(2)}, u32[]{:S(2)}) collective-permute-start(bf16[128,2048]{1,0:T(8,128)(2,1)S(1)} %get-tuple-element.93), channel_id=1, source_target_pairs={{0,8},{8,0},{16,24},{24,16},{32,40},{40,32},{48,56},{56,48},{64,72... | collective-permute-start | bytes 1572872 | tf_op jit(solution)/shard_map/ppermute | solution.py:401
  14.2 12.9 %collective-permute-start.5 = (bf16[64,2048]{1,0:T(8,128)(2,1)S(1)}, bf16[64,2048]{1,0:T(8,128)(2,1)S(1)}, u32[]{:S(2)}, u32[]{:S(2)}) collective-permute-start(bf16[64,2048]{1,0:T(8,128)(2,1)S(1)} %get-tuple-element.94), channel_id=1, source_target_pairs={{0,24},{8,16},{16,8},{24,0},{32,56},{40,48},{48,40},{56,32},{64,88... | collective-permute-start | bytes 786440 | tf_op jit(solution)/shard_map/ppermute | solution.py:403
  15.7 14.1 %collective-permute-start.4 = (bf16[64,2048]{1,0:T(8,128)(2,1)S(1)}, bf16[64,2048]{1,0:T(8,128)(2,1)S(1)}, u32[]{:S(2)}, u32[]{:S(2)}) collective-permute-start(bf16[64,2048]{1,0:T(8,128)(2,1)S(1)} %get-tuple-element.94), channel_id=1, source_target_pairs={{0,16},{8,24},{16,8},{24,0},{32,48},{40,56},{48,40},{56,32},{64,80... | collective-permute-start | bytes 786440 | tf_op jit(solution)/shard_map/ppermute | solution.py:402
  16.9 7.2 %collective-permute-start.6 = (bf16[32,512]{1,0:T(8,128)(2,1)S(1)}, bf16[32,512]{1,0:T(8,128)(2,1)S(1)}, u32[]{:S(2)}, u32[]{:S(2)}) collective-permute-start(bf16[32,512]{1,0:T(8,128)(2,1)S(1)} %get-tuple-element.90), channel_id=1, source_target_pairs={{0,224},{8,232},{16,240},{24,248},{32,192},{40,200},{48,208},{56,2... | collective-permute-start | bytes 98312 | tf_op jit(solution)/shard_map/ppermute | solution.py:398
  24.1 12.1 %collective-permute-start.7 = (bf16[160,512]{1,0:T(8,128)(2,1)S(1)}, bf16[160,512]{1,0:T(8,128)(2,1)S(1)}, u32[]{:S(2)}, u32[]{:S(2)}) collective-permute-start(bf16[160,512]{1,0:T(8,128)(2,1)S(1)} %get-tuple-element.100), channel_id=1, source_target_pairs={{0,32},{8,40},{16,48},{24,56},{32,0},{40,8},{48,16},{56,24},{64,96... | collective-permute-start | bytes 491528 | tf_op jit(solution)/shard_map/ppermute | solution.py:415
  25.5 5.6 %collective-permute-start.9 = (bf16[96,512]{1,0:T(8,128)(2,1)S(1)}, bf16[96,512]{1,0:T(8,128)(2,1)S(1)}, u32[]{:S(2)}, u32[]{:S(2)}) collective-permute-start(bf16[96,512]{1,0:T(8,128)(2,1)S(1)} %get-tuple-element.101), channel_id=1, source_target_pairs={{0,96},{8,104},{16,112},{24,120},{32,64},{40,72},{48,80},{56,88},{... | collective-permute-start | bytes 294920 | tf_op jit(solution)/shard_map/ppermute | solution.py:414
  27.1 9.0 %collective-permute-start.8 = (bf16[96,512]{1,0:T(8,128)(2,1)S(1)}, bf16[96,512]{1,0:T(8,128)(2,1)S(1)}, u32[]{:S(2)}, u32[]{:S(2)}) collective-permute-start(bf16[96,512]{1,0:T(8,128)(2,1)S(1)} %get-tuple-element.101), channel_id=1, source_target_pairs={{0,64},{8,72},{16,80},{24,88},{32,96},{40,104},{48,112},{56,120},{... | collective-permute-start | bytes 294920 | tf_op jit(solution)/shard_map/ppermute | solution.py:413
  37.1 11.7 %collective-permute-start.10 = (bf16[4,512,512]{2,1,0:T(8,128)(2,1)S(1)}, bf16[4,512,512]{2,1,0:T(8,128)(2,1)S(1)}, u32[]{:S(2)}, u32[]{:S(2)}) collective-permute-start(bf16[4,512,512]{2,1,0:T(8,128)(2,1)S(1)} %get-tuple-element.104), channel_id=1, source_target_pairs={{0,1},{1,0},{2,3},{3,2},{4,5},{5,4},{6,7},{7,6},{8,9},{9,8},{10,11... | collective-permute-start | bytes 6291464 | tf_op jit(solution)/shard_map/ppermute | solution.py:429
  39.1 5.9 %collective-permute-start.11 = (bf16[32,384]{1,0:T(8,128)(2,1)S(1)}, bf16[32,384]{1,0:T(8,128)(2,1)S(1)}, u32[]{:S(2)}, u32[]{:S(2)}) collective-permute-start(bf16[32,384]{1,0:T(8,128)(2,1)S(1)} %get-tuple-element.102), channel_id=1, source_target_pairs={{0,8},{8,16},{16,24},{24,0},{32,40},{40,48},{48,56},{56,32},{64,72... | collective-permute-start | bytes 73736 | tf_op jit(solution)/shard_map/ppermute | solution.py:430
  39.6 5.0 %collective-permute-start.12 = (bf16[32,384]{1,0:T(8,128)(2,1)S(1)}, bf16[32,384]{1,0:T(8,128)(2,1)S(1)}, u32[]{:S(2)}, u32[]{:S(2)}) collective-permute-start(bf16[32,384]{1,0:T(8,128)(2,1)S(1)} %get-tuple-element.106), channel_id=1, source_target_pairs={{0,16},{8,24},{16,0},{24,8},{32,48},{40,56},{48,32},{56,40},{64,80... | collective-permute-start | bytes 73736 | tf_op jit(solution)/shard_map/ppermute | solution.py:432
  41.7 3.2 %collective-permute-start.13 = (bf16[32,384]{1,0:T(8,128)(2,1)S(1)}, bf16[32,384]{1,0:T(8,128)(2,1)S(1)}, u32[]{:S(2)}, u32[]{:S(2)}) collective-permute-start(bf16[32,384]{1,0:T(8,128)(2,1)S(1)} %get-tuple-element.107), channel_id=1, source_target_pairs={{0,24},{8,0},{16,8},{24,16},{32,56},{40,32},{48,40},{56,48},{64,88... | collective-permute-start | bytes 73736 | tf_op jit(solution)/shard_map/ppermute | solution.py:431
  46.0 2.9 %collective-permute-start.14 = (bf16[512,512]{1,0:T(8,128)(2,1)S(1)}, bf16[512,512]{1,0:T(8,128)(2,1)S(1)}, u32[]{:S(2)}, u32[]{:S(2)}) collective-permute-start(bf16[512,512]{1,0:T(8,128)(2,1)S(1)} %finish.1.a1), channel_id=1, source_target_pairs={{0,1},{1,0},{2,3},{3,2},{4,5},{5,4},{6,7},{7,6},{8,9},{9,8},{10,11... | collective-permute-start | bytes 1572872 | tf_op jit(solution)/shard_map/ppermute | solution.py:455
  49.6 8.1 %collective-permute-start.16 = (bf16[256,512]{1,0:T(8,128)(2,1)S(1)}, bf16[256,512]{1,0:T(8,128)(2,1)S(1)}, u32[]{:S(2)}, u32[]{:S(2)}) collective-permute-start(bf16[256,512]{1,0:T(8,128)(2,1)S(1)} %get-tuple-element.132), channel_id=1, source_target_pairs={{0,6},{1,7},{2,0},{3,1},{4,2},{5,3},{6,4},{7,5},{8,14},{9,15},{10,... | collective-permute-start | bytes 786440 | tf_op jit(solution)/shard_map/ppermute | solution.py:474
  52.4 8.4 %collective-permute-start.15 = (bf16[256,512]{1,0:T(8,128)(2,1)S(1)}, bf16[256,512]{1,0:T(8,128)(2,1)S(1)}, u32[]{:S(2)}, u32[]{:S(2)}) collective-permute-start(bf16[256,512]{1,0:T(8,128)(2,1)S(1)} %get-tuple-element.123), channel_id=1, source_target_pairs={{0,2},{1,3},{2,4},{3,5},{4,6},{5,7},{6,0},{7,1},{8,10},{9,11},{10,... | collective-permute-start | bytes 786440 | tf_op jit(solution)/shard_map/ppermute | solution.py:473
  53.2 13.3 %collective-permute-start.19 = (bf16[256,512]{1,0:T(8,128)(2,1)S(1)}, bf16[256,512]{1,0:T(8,128)(2,1)S(1)}, u32[]{:S(2)}, u32[]{:S(2)}) collective-permute-start(bf16[256,512]{1,0:T(8,128)(2,1)S(1)} %get-tuple-element.126), channel_id=1, source_target_pairs={{0,2},{1,3},{2,4},{3,5},{4,6},{5,7},{6,0},{7,1},{8,10},{9,11},{10,... | collective-permute-start | bytes 786440 | tf_op jit(solution)/shard_map/ppermute | solution.py:486
  53.3 10.4 %collective-permute-start.18 = (bf16[256,512]{1,0:T(8,128)(2,1)S(1)}, bf16[256,512]{1,0:T(8,128)(2,1)S(1)}, u32[]{:S(2)}, u32[]{:S(2)}) collective-permute-start(bf16[256,512]{1,0:T(8,128)(2,1)S(1)} %get-tuple-element.134), channel_id=1, source_target_pairs={{0,6},{1,7},{2,0},{3,1},{4,2},{5,3},{6,4},{7,5},{8,14},{9,15},{10,... | collective-permute-start | bytes 786440 | tf_op jit(solution)/shard_map/ppermute | solution.py:487
  60.9 11.1 %collective-permute-start.17 = (bf16[256,512]{1,0:T(8,128)(2,1)S(1)}, bf16[256,512]{1,0:T(8,128)(2,1)S(1)}, u32[]{:S(2)}, u32[]{:S(2)}) collective-permute-start(bf16[256,512]{1,0:T(8,128)(2,1)S(1)} %get-tuple-element.133), channel_id=1, source_target_pairs={{0,2},{1,3},{2,4},{3,5},{4,6},{5,7},{6,0},{7,1},{8,10},{9,11},{10,... | collective-permute-start | bytes 786440 | tf_op jit(solution)/shard_map/ppermute | solution.py:502
  61.0 11.1 %collective-permute-start.20 = (bf16[256,512]{1,0:T(8,128)(2,1)S(1)}, bf16[256,512]{1,0:T(8,128)(2,1)S(1)}, u32[]{:S(2)}, u32[]{:S(2)}) collective-permute-start(bf16[256,512]{1,0:T(8,128)(2,1)S(1)} %get-tuple-element.135), channel_id=1, source_target_pairs={{0,6},{1,7},{2,0},{3,1},{4,2},{5,3},{6,4},{7,5},{8,14},{9,15},{10,... | collective-permute-start | bytes 786440 | tf_op jit(solution)/shard_map/ppermute | solution.py:503
  (5 other events, 26.9 us)
where the time goes:
time: 73.1 us; the launch traced here: 72.9 us
  starting transfers between devices  32.2 us (44%)
  waiting for transfers between devices  24.3 us (33%)
  Pallas kernels  15.2 us (21%)
  between operations  0.86 us (1%)
    ppermute x1, waiting for transfers between devices, on_device(): from_down_a = lax.ppermute(send_up, 'head', y_route(1))  5.62 us
    ppermute x1, starting transfers between devices, on_device(): g4 = lax.ppermute(k5, 'ctx', z_route(7))  5.58 us
    ppermute x1, waiting for transfers between devices, on_device(): g2 = lax.ppermute(two, 'ctx', z_route(2))  5.02 us
    ppermute x1, starting transfers between devices, on_device(): t2 = lax.ppermute(t2, 'ctx', x_route(2))  3.66 us
    ppermute x1, waiting for transfers between devices, on_device(): got_a = lax.ppermute(far_a, 'head', y_route(1))  3.09 us
    ppermute x1, starting transfers between devices, on_device(): got_b = lax.ppermute(far_b, 'head', y_route(3))  2.82 us
    pallas_call x1, Pallas kernels, on_device(): call(lift_kernel, (level3,) * 4, [HBM] * 6, 'lift', 10 ** 9, 2 * 2 ** 20,...  2.79 us
    ppermute x1, waiting for transfers between devices, on_device(): from_down_b = lax.ppermute(up_b, 'head', y_route(1))  2.77 us
  transfers between devices with their start and end apart: 21, of which 10 were waited for; matrix products, arithmetic and copies ran while one was open for 0% of the time, Pallas kernels for 13%

commit v1 on v0

--- a/solution.py
+++ b/solution.py
@@ -249,25 +249,25 @@
         (other if flip else mine)[step] = landed[num].T
 
 
-def project(w1, w2, a1, a2):
-    return dot_nt(w1, a1[...]) + dot_nt(w2, a2[...])
-
-
-def far_chunk_kernel(w1, w2, a1, a2, half_a, half_b):
-    both = project(w1[0], w2[0], a1, a2).astype(BF16)
-    half_a[...] = both[:256]
-    half_b[...] = both[256:]
-
-
-def near_chunk_kernel(u1, u2, d1, d2, a1, a2, up_b, down_a):
-    up_b[...] = project(u1[0, 256:], u2[0, 256:], a1, a2).astype(BF16)
-    down_a[...] = project(d1[0, :256], d2[0, :256], a1, a2).astype(BF16)
-
-
-def own_chunk_kernel(u1, u2, d1, d2, m1, m2, a1, a2, up_a, down_b, own):
-    up_a[...] = project(u1[0, :256], u2[0, :256], a1, a2)
-    down_b[...] = project(d1[0, 256:], d2[0, 256:], a1, a2)
-    own[...] = project(m1[0], m2[0], a1, a2)
+def begin_kernel(w_mine, mine, part):
+    for step in (2, 1, 3, 0):
+        part[step] = dot_nt(w_mine[step], mine[...])
+
+
+def far_chunk_kernel(w, part, pair, half_a, half_b):
+    half_a[...] = (part[0, :256] + dot_nt(w[0, :256], pair[...])).astype(BF16)
+    half_b[...] = (part[0, 256:] + dot_nt(w[0, 256:], pair[...])).astype(BF16)
+
+
+def near_chunk_kernel(wu, wd, pu, pd, pair, up_b, down_a):
+    up_b[...] = (pu[0, 256:] + dot_nt(wu[0, 256:], pair[...])).astype(BF16)
+    down_a[...] = (pd[0, :256] + dot_nt(wd[0, :256], pair[...])).astype(BF16)
+
+
+def own_chunk_kernel(wu, wd, wm, pu, pd, pm, pair, up_a, down_b, own):
+    up_a[...] = pu[0, :256] + dot_nt(wu[0, :256], pair[...])
+    down_b[...] = pd[0, 256:] + dot_nt(wd[0, 256:], pair[...])
+    own[...] = pm[0] + dot_nt(wm[0], pair[...])
 
 
 def relay_kernel(up_a, got_a, down_b, got_b, send_up, send_down):
@@ -453,6 +453,14 @@
         scratch=[pltpu.VMEM((4, 256, HD), F32)],
     )(s0, b1, b2, b3, *leaf)
     pair = lax.ppermute(mine, "head", core_route())
+    part = call(
+        begin_kernel,
+        shape((NY, 512, rows), F32),
+        [VMEM] * 2,
+        "chunk_begin",
+        10**9,
+        6 * 2**20,
+    )(w_mine, mine)
 
     def chunk(j):
         return pl.BlockSpec((1, 512, 512), lambda i, j=j: (j, 0, 0))
@@ -463,39 +471,39 @@
     far_a, far_b = call(
         far_chunk_kernel,
         (shape((256, rows)),) * 2,
-        [chunk(2)] * 2 + [whole] * 2,
+        [chunk(2)] * 2 + [whole],
         "chunk_far",
         5 * 10**8,
         2 * 2**20,
         out_specs=(half,) * 2,
         grid=(1,),
-    )(w_mine, w_pair, mine, pair)
+    )(w_pair, part, pair)
     got_a = lax.ppermute(far_a, "head", y_route(1))
     got_b = lax.ppermute(far_b, "head", y_route(3))
-    _, mine2, pair2 = after(far_a, mine, pair)
+    _, part2, pair2 = after(far_a, part, pair)
     up_b, down_a = call(
         near_chunk_kernel,
         (shape((256, rows)),) * 2,
-        [chunk(1)] * 2 + [chunk(3)] * 2 + [whole] * 2,
+        [chunk(1), chunk(3)] * 2 + [whole],
         "chunk_near",
         5 * 10**8,
         3 * 2**20,
         out_specs=(half,) * 2,
         grid=(1,),
-    )(w_mine, w_pair, w_mine, w_pair, mine2, pair2)
+    )(w_pair, w_pair, part2, part2, pair2)
     from_down_b = lax.ppermute(up_b, "head", y_route(1))
     from_up_a = lax.ppermute(down_a, "head", y_route(3))
-    _, mine3, pair3 = after(up_b, mine, pair)
+    _, part3, pair3 = after(up_b, part, pair)
     up_a, down_b, own = call(
         own_chunk_kernel,
         (shape((256, rows), F32),) * 2 + (shape((512, rows), F32),),
-        [chunk(1)] * 2 + [chunk(3)] * 2 + [chunk(0)] * 2 + [whole] * 2,
+        [chunk(1), chunk(3), chunk(0)] * 2 + [whole],
         "chunk_own",
         10**9,
         5 * 2**20,
         out_specs=(half, half, full),
         grid=(1,),
-    )(w_mine, w_pair, w_mine, w_pair, w_mine, w_pair, mine3, pair3)
+    )(w_pair, w_pair, w_pair, part3, part3, part3, pair3)
     send_up, send_down = call(
         relay_kernel, (shape((256, rows)),) * 2, [VMEM] * 4, "relay", 10**6, 2 * 2**20
     )(up_a, got_a, down_b, got_b)

time: 73.1 us -> 72.8 us (level)
    ppermute x1, waiting for transfers between devices: 1.54 us -> 0.25 us  [on_device(): pair = lax.ppermute(mine, 'head', core_route())]
    pallas_call x1 -> x2, Pallas kernels: 0.73 us -> 1.75 us  [the longest x1 1.28 us: on_device(): call(begin_kernel, shape((NY, 512, rows), F32), [VMEM] * 2, 'chunk_begin'...]
    ppermute x1, waiting for transfers between devices: 0.44 us -> 1.25 us  [on_device(): got_b = lax.ppermute(far_b, 'head', y_route(3))]
  transfers between devices with their start and end apart: 21 -> 21, of which waited for: 10 -> 10; matrix products, arithmetic and copies ran while one was open for 0% -> 0% of each run, Pallas kernels for 13% -> 14%
where the time goes in v1:
time: 72.8 us; the launch traced here: 72.7 us
  starting transfers between devices  32.2 us (44%)
  waiting for transfers between devices  23.9 us (33%)
  Pallas kernels  15.4 us (21%)
  between operations  0.86 us (1%)
    ppermute x1, waiting for transfers between devices, on_device(): from_down_a = lax.ppermute(send_up, 'head', y_route(1))  5.62 us
    ppermute x1, starting transfers between devices, on_device(): g4 = lax.ppermute(k5, 'ctx', z_route(7))  5.58 us
    ppermute x1, waiting for transfers between devices, on_device(): g2 = lax.ppermute(two, 'ctx', z_route(2))  5.02 us
    ppermute x1, starting transfers between devices, on_device(): t2 = lax.ppermute(t2, 'ctx', x_route(2))  3.66 us
    ppermute x1, waiting for transfers between devices, on_device(): got_a = lax.ppermute(far_a, 'head', y_route(1))  3.09 us
    ppermute x1, starting transfers between devices, on_device(): got_b = lax.ppermute(far_b, 'head', y_route(3))  2.82 us
    pallas_call x1, Pallas kernels, on_device(): call(lift_kernel, (level3,) * 4, [HBM] * 6, 'lift', 10 ** 9, 2 * 2 ** 20,...  2.79 us
    ppermute x1, waiting for transfers between devices, on_device(): from_down_b = lax.ppermute(up_b, 'head', y_route(1))  2.77 us
  transfers between devices with their start and end apart: 21, of which 10 were waited for; matrix products, arithmetic and copies ran while one was open for 0% of the time, Pallas kernels for 14%

profile of v1, /device:TPU:1, one launch (start us, length us, event | category | flops | bytes accessed | tf_op | source)
XLA Modules:
  0.0 72.7 jit_solution(5718026764997665425)
XLA Ops:
  0.7 2.8 %lift.1 = (bf16[32,768]{1,0:T(8,128)(2,1)}, bf16[32,768]{1,0:T(8,128)(2,1)}, bf16[32,768]{1,0:T(8,128)(2,1)}, bf16[32,768]{1,0:T(8,128)(2,1)}) custom-call(bf16[256,512]{1,0:T(8,128)(2,1)} %q.3, bf16[256,512]{1,0:T(8,128)(2,1)} %tq.3, bf16[256,512]{1,0:T(8,128)(2,1)} %tk.3, bf16[256,512]{1,0:T(8,128)(2,1)} %k.3, bf16[256,512]{1,0:T(8,128)(2,1)} %v.3, ...), custom_call_target="tpu_custom_call" | custom-call | flops 1000000000 | bytes 2097152 | tf_op jit(solution)/shard_map/lift/pallas_call | solution.py:333
  3.5 3.7 %collective-permute-start.1 = (bf16[32,768]{1,0:T(8,128)(2,1)}, bf16[32,768]{1,0:T(8,128)(2,1)S(1)}, u32[]{:S(2)}, u32[]{:S(2)}) collective-permute-start(bf16[32,768]{1,0:T(8,128)(2,1)} %get-tuple-element.86), channel_id=1, source_target_pairs={{0,16},{8,24},{16,0},{24,8},{32,48},{40,56},{48,32},{56,40},{64,80... | collective-permute-start | bytes 147464 | tf_op jit(solution)/shard_map/ppermute | solution.py:364
  8.7 1.4 %leaf.1 = (f32[4,256,128]{2,1,0:T(8,128)S(1)}, f32[4,256,128]{2,1,0:T(8,128)S(1)}, f32[4,256,128]{2,1,0:T(8,128)S(1)}) custom-call(bf16[256,512]{1,0:T(8,128)(2,1)S(1)} %copy-done.1, bf16[256,512]{1,0:T(8,128)(2,1)S(1)} %copy-done.2, bf16[256,512]{1,0:T(8,128)(2,1)S(1)} %copy-done.3, bf16[256,512]{1,0:T(8,128)(2,1)S(1)} %copy-done.4, ...), custom_call_target="tpu_custom_call" | custom-call | flops 2000000000 | bytes 5242880 | tf_op jit(solution)/shard_map/leaf/pallas_call | solution.py:367
  10.2 2.2 %weights.1 = (bf16[4,512,512]{2,1,0:T(8,128)(2,1)S(1)}, bf16[4,512,512]{2,1,0:T(8,128)(2,1)S(1)}) custom-call(bf16[512,4096]{1,0:T(8,128)(2,1)S(1)} %copy-done), custom_call_target="tpu_custom_call" | custom-call | flops 1000000 | bytes 12582912 | tf_op jit(solution)/shard_map/weights/pallas_call | solution.py:377
  14.2 1.5 %collective-permute-start.5 = (bf16[64,2048]{1,0:T(8,128)(2,1)S(1)}, bf16[64,2048]{1,0:T(8,128)(2,1)S(1)}, u32[]{:S(2)}, u32[]{:S(2)}) collective-permute-start(bf16[64,2048]{1,0:T(8,128)(2,1)S(1)} %get-tuple-element.93), channel_id=1, source_target_pairs={{0,24},{8,16},{16,8},{24,0},{32,56},{40,48},{48,40},{56,32},{64,88... | collective-permute-start | bytes 786440 | tf_op jit(solution)/shard_map/ppermute | solution.py:403
  16.9 5.6 %collective-permute-start.6 = (bf16[32,512]{1,0:T(8,128)(2,1)S(1)}, bf16[32,512]{1,0:T(8,128)(2,1)S(1)}, u32[]{:S(2)}, u32[]{:S(2)}) collective-permute-start(bf16[32,512]{1,0:T(8,128)(2,1)S(1)} %get-tuple-element.89), channel_id=1, source_target_pairs={{0,224},{8,232},{16,240},{24,248},{32,192},{40,200},{48,208},{56,2... | collective-permute-start | bytes 98312 | tf_op jit(solution)/shard_map/ppermute | solution.py:398
  22.5 1.6 %collective-permute-done.6.g4 = bf16[32,512]{1,0:T(8,128)(2,1)S(1)} collective-permute-done((bf16[32,512]{1,0:T(8,128)(2,1)S(1)}, bf16[32,512]{1,0:T(8,128)(2,1)S(1)}, u32[]{:S(2)}, u32[]{:S(2)}) %collective-permute-start.6) | collective-permute-done | bytes 32800 | tf_op jit(solution)/shard_map/ppermute | solution.py:398
  24.1 1.4 %collective-permute-start.7 = (bf16[160,512]{1,0:T(8,128)(2,1)S(1)}, bf16[160,512]{1,0:T(8,128)(2,1)S(1)}, u32[]{:S(2)}, u32[]{:S(2)}) collective-permute-start(bf16[160,512]{1,0:T(8,128)(2,1)S(1)} %get-tuple-element.99), channel_id=1, source_target_pairs={{0,32},{8,40},{16,48},{24,56},{32,0},{40,8},{48,16},{56,24},{64,96... | collective-permute-start | bytes 491528 | tf_op jit(solution)/shard_map/ppermute | solution.py:415
  25.5 1.6 %collective-permute-start.9 = (bf16[96,512]{1,0:T(8,128)(2,1)S(1)}, bf16[96,512]{1,0:T(8,128)(2,1)S(1)}, u32[]{:S(2)}, u32[]{:S(2)}) collective-permute-start(bf16[96,512]{1,0:T(8,128)(2,1)S(1)} %get-tuple-element.100), channel_id=1, source_target_pairs={{0,96},{8,104},{16,112},{24,120},{32,64},{40,72},{48,80},{56,88},{... | collective-permute-start | bytes 294920 | tf_op jit(solution)/shard_map/ppermute | solution.py:414
  27.1 2.7 %collective-permute-done.4.c2 = bf16[64,2048]{1,0:T(8,128)(2,1)S(1)} collective-permute-done((bf16[64,2048]{1,0:T(8,128)(2,1)S(1)}, bf16[64,2048]{1,0:T(8,128)(2,1)S(1)}, u32[]{:S(2)}, u32[]{:S(2)}) %collective-permute-start.4) | collective-permute-done | bytes 262176 | tf_op jit(solution)/shard_map/ppermute | solution.py:402
  29.8 1.3 %collective-permute-done.9.g3 = bf16[96,512]{1,0:T(8,128)(2,1)S(1)} collective-permute-done((bf16[96,512]{1,0:T(8,128)(2,1)S(1)}, bf16[96,512]{1,0:T(8,128)(2,1)S(1)}, u32[]{:S(2)}, u32[]{:S(2)}) %collective-permute-start.9) | collective-permute-done | bytes 98336 | tf_op jit(solution)/shard_map/ppermute | solution.py:414
  31.1 5.0 %collective-permute-done.8.g2 = bf16[96,512]{1,0:T(8,128)(2,1)S(1)} collective-permute-done((bf16[96,512]{1,0:T(8,128)(2,1)S(1)}, bf16[96,512]{1,0:T(8,128)(2,1)S(1)}, u32[]{:S(2)}, u32[]{:S(2)}) %collective-permute-start.8) | collective-permute-done | bytes 98336 | tf_op jit(solution)/shard_map/ppermute | solution.py:413
  37.1 1.9 %collective-permute-start.10 = (bf16[4,512,512]{2,1,0:T(8,128)(2,1)S(1)}, bf16[4,512,512]{2,1,0:T(8,128)(2,1)S(1)}, u32[]{:S(2)}, u32[]{:S(2)}) collective-permute-start(bf16[4,512,512]{2,1,0:T(8,128)(2,1)S(1)} %get-tuple-element.103), channel_id=1, source_target_pairs={{0,1},{1,0},{2,3},{3,2},{4,5},{5,4},{6,7},{7,6},{8,9},{9,8},{10,11... | collective-permute-start | bytes 6291464 | tf_op jit(solution)/shard_map/ppermute | solution.py:429
  39.6 2.0 %collective-permute-start.12 = (bf16[32,384]{1,0:T(8,128)(2,1)S(1)}, bf16[32,384]{1,0:T(8,128)(2,1)S(1)}, u32[]{:S(2)}, u32[]{:S(2)}) collective-permute-start(bf16[32,384]{1,0:T(8,128)(2,1)S(1)} %get-tuple-element.106), channel_id=1, source_target_pairs={{0,16},{8,24},{16,0},{24,8},{32,48},{40,56},{48,32},{56,40},{64,80... | collective-permute-start | bytes 73736 | tf_op jit(solution)/shard_map/ppermute | solution.py:432
  42.5 2.2 %home.1 = (f32[4,256,128]{2,1,0:T(8,128)S(1)}, f32[4,256,128]{2,1,0:T(8,128)S(1)}, f32[4,256,128]{2,1,0:T(8,128)S(1)}) custom-call(bf16[128,1024]{1,0:T(8,128)(2,1)S(1)} %get-tuple-element.112.q1, bf16[64,1024]{1,0:T(8,128)(2,1)S(1)} %get-tuple-element.113.q2, bf16[128,2048]{1,0:T(8,128)(2,1)S(1)} %collective-permute-done.3.c1, ...), custom_call_target="tpu_custom_call" | custom-call | flops 2000000000 | bytes 4194304 | tf_op jit(solution)/shard_map/home/pallas_call | solution.py:435
  46.0 1.3 %collective-permute-start.14 = (bf16[512,512]{1,0:T(8,128)(2,1)S(1)}, bf16[512,512]{1,0:T(8,128)(2,1)S(1)}, u32[]{:S(2)}, u32[]{:S(2)}) collective-permute-start(bf16[512,512]{1,0:T(8,128)(2,1)S(1)} %finish.1.mine), channel_id=1, source_target_pairs={{0,1},{1,0},{2,3},{3,2},{4,5},{5,4},{6,7},{7,6},{8,9},{9,8},{10,11... | collective-permute-start | bytes 1572872 | tf_op jit(solution)/shard_map/ppermute | solution.py:455
  47.3 1.3 %chunk_begin.1.part.pu.pd.pm = f32[4,512,512]{2,1,0:T(8,128)S(1)} custom-call(bf16[4,512,512]{2,1,0:T(8,128)(2,1)S(1)} %get-tuple-element.104.w_mine, bf16[512,512]{1,0:T(8,128)(2,1)S(1)} %finish.1.mine), custom_call_target="tpu_custom_call" | custom-call | flops 1000000000 | bytes 6291456 | tf_op jit(solution)/shard_map/chunk_begin/pallas_call | solution.py:456
  49.3 2.8 %collective-permute-start.16 = (bf16[256,512]{1,0:T(8,128)(2,1)S(1)}, bf16[256,512]{1,0:T(8,128)(2,1)S(1)}, u32[]{:S(2)}, u32[]{:S(2)}) collective-permute-start(bf16[256,512]{1,0:T(8,128)(2,1)S(1)} %get-tuple-element.132), channel_id=1, source_target_pairs={{0,6},{1,7},{2,0},{3,1},{4,2},{5,3},{6,4},{7,5},{8,14},{9,15},{10,... | collective-permute-start | bytes 786440 | tf_op jit(solution)/shard_map/ppermute | solution.py:482
  52.7 2.7 %collective-permute-start.18 = (bf16[256,512]{1,0:T(8,128)(2,1)S(1)}, bf16[256,512]{1,0:T(8,128)(2,1)S(1)}, u32[]{:S(2)}, u32[]{:S(2)}) collective-permute-start(bf16[256,512]{1,0:T(8,128)(2,1)S(1)} %get-tuple-element.134), channel_id=1, source_target_pairs={{0,6},{1,7},{2,0},{3,1},{4,2},{5,3},{6,4},{7,5},{8,14},{9,15},{10,... | collective-permute-start | bytes 786440 | tf_op jit(solution)/shard_map/ppermute | solution.py:495
  56.2 1.3 %collective-permute-done.16.got_b = bf16[256,512]{1,0:T(8,128)(2,1)S(1)} collective-permute-done((bf16[256,512]{1,0:T(8,128)(2,1)S(1)}, bf16[256,512]{1,0:T(8,128)(2,1)S(1)}, u32[]{:S(2)}, u32[]{:S(2)}) %collective-permute-start.16) | collective-permute-done | bytes 262176 | tf_op jit(solution)/shard_map/ppermute | solution.py:482
  57.5 3.1 %collective-permute-done.15.got_a = bf16[256,512]{1,0:T(8,128)(2,1)S(1)} collective-permute-done((bf16[256,512]{1,0:T(8,128)(2,1)S(1)}, bf16[256,512]{1,0:T(8,128)(2,1)S(1)}, u32[]{:S(2)}, u32[]{:S(2)}) %collective-permute-start.15) | collective-permute-done | bytes 262176 | tf_op jit(solution)/shard_map/ppermute | solution.py:481
  60.7 2.7 %collective-permute-start.20 = (bf16[256,512]{1,0:T(8,128)(2,1)S(1)}, bf16[256,512]{1,0:T(8,128)(2,1)S(1)}, u32[]{:S(2)}, u32[]{:S(2)}) collective-permute-start(bf16[256,512]{1,0:T(8,128)(2,1)S(1)} %get-tuple-element.135), channel_id=1, source_target_pairs={{0,6},{1,7},{2,0},{3,1},{4,2},{5,3},{6,4},{7,5},{8,14},{9,15},{10,... | collective-permute-start | bytes 786440 | tf_op jit(solution)/shard_map/ppermute | solution.py:511
  63.4 2.8 %collective-permute-done.19.from_down_b = bf16[256,512]{1,0:T(8,128)(2,1)S(1)} collective-permute-done((bf16[256,512]{1,0:T(8,128)(2,1)S(1)}, bf16[256,512]{1,0:T(8,128)(2,1)S(1)}, u32[]{:S(2)}, u32[]{:S(2)}) %collective-permute-start.19) | collective-permute-done | bytes 262176 | tf_op jit(solution)/shard_map/ppermute | solution.py:494
  66.2 5.6 %collective-permute-done.17.from_down_a = bf16[256,512]{1,0:T(8,128)(2,1)S(1)} collective-permute-done((bf16[256,512]{1,0:T(8,128)(2,1)S(1)}, bf16[256,512]{1,0:T(8,128)(2,1)S(1)}, u32[]{:S(2)}, u32[]{:S(2)}) %collective-permute-start.17) | collective-permute-done | bytes 262176 | tf_op jit(solution)/shard_map/ppermute | solution.py:510
  (49 shorter events, 11.4 us)
Async XLA Ops:
  0.6 8.0 %copy-start.6 = (bf16[256,512]{1,0:T(8,128)(2,1)S(1)}, bf16[256,512]{1,0:T(8,128)(2,1)}, u32[]{:S(2)}) copy-start(bf16[256,512]{1,0:T(8,128)(2,1)} %tv.3) | copy-start | bytes 786436
  0.6 8.0 %copy-start.3 = (bf16[256,512]{1,0:T(8,128)(2,1)S(1)}, bf16[256,512]{1,0:T(8,128)(2,1)}, u32[]{:S(2)}) copy-start(bf16[256,512]{1,0:T(8,128)(2,1)} %tk.3) | copy-start | bytes 786436
  0.7 8.0 %copy-start.2 = (bf16[256,512]{1,0:T(8,128)(2,1)S(1)}, bf16[256,512]{1,0:T(8,128)(2,1)}, u32[]{:S(2)}) copy-start(bf16[256,512]{1,0:T(8,128)(2,1)} %tq.3) | copy-start | bytes 786436
  3.5 9.6 %collective-permute-start.1 = (bf16[32,768]{1,0:T(8,128)(2,1)}, bf16[32,768]{1,0:T(8,128)(2,1)S(1)}, u32[]{:S(2)}, u32[]{:S(2)}) collective-permute-start(bf16[32,768]{1,0:T(8,128)(2,1)} %get-tuple-element.86), channel_id=1, source_target_pairs={{0,16},{8,24},{16,0},{24,8},{32,48},{40,56},{48,32},{56,40},{64,80... | collective-permute-start | bytes 147464 | tf_op jit(solution)/shard_map/ppermute | solution.py:364
  7.1 5.9 %collective-permute-start.2 = (bf16[32,768]{1,0:T(8,128)(2,1)}, bf16[32,768]{1,0:T(8,128)(2,1)S(1)}, u32[]{:S(2)}, u32[]{:S(2)}) collective-permute-start(bf16[32,768]{1,0:T(8,128)(2,1)} %get-tuple-element.87), channel_id=1, source_target_pairs={{0,24},{8,0},{16,8},{24,16},{32,56},{40,32},{48,40},{56,48},{64,88... | collective-permute-start | bytes 147464 | tf_op jit(solution)/shard_map/ppermute | solution.py:363
  8.0 5.1 %collective-permute-start = (bf16[32,768]{1,0:T(8,128)(2,1)}, bf16[32,768]{1,0:T(8,128)(2,1)S(1)}, u32[]{:S(2)}, u32[]{:S(2)}) collective-permute-start(bf16[32,768]{1,0:T(8,128)(2,1)} %get-tuple-element.70), channel_id=1, source_target_pairs={{0,8},{8,16},{16,24},{24,0},{32,40},{40,48},{48,56},{56,32},{64,72... | collective-permute-start | bytes 147464 | tf_op jit(solution)/shard_map/ppermute | solution.py:362
  13.5 16.3 %collective-permute-start.3 = (bf16[128,2048]{1,0:T(8,128)(2,1)S(1)}, bf16[128,2048]{1,0:T(8,128)(2,1)S(1)}, u32[]{:S(2)}, u32[]{:S(2)}) collective-permute-start(bf16[128,2048]{1,0:T(8,128)(2,1)S(1)} %get-tuple-element.92), channel_id=1, source_target_pairs={{0,8},{8,0},{16,24},{24,16},{32,40},{40,32},{48,56},{56,48},{64,72... | collective-permute-start | bytes 1572872 | tf_op jit(solution)/shard_map/ppermute | solution.py:401
  14.2 12.9 %collective-permute-start.5 = (bf16[64,2048]{1,0:T(8,128)(2,1)S(1)}, bf16[64,2048]{1,0:T(8,128)(2,1)S(1)}, u32[]{:S(2)}, u32[]{:S(2)}) collective-permute-start(bf16[64,2048]{1,0:T(8,128)(2,1)S(1)} %get-tuple-element.93), channel_id=1, source_target_pairs={{0,24},{8,16},{16,8},{24,0},{32,56},{40,48},{48,40},{56,32},{64,88... | collective-permute-start | bytes 786440 | tf_op jit(solution)/shard_map/ppermute | solution.py:403
  15.7 14.1 %collective-permute-start.4 = (bf16[64,2048]{1,0:T(8,128)(2,1)S(1)}, bf16[64,2048]{1,0:T(8,128)(2,1)S(1)}, u32[]{:S(2)}, u32[]{:S(2)}) collective-permute-start(bf16[64,2048]{1,0:T(8,128)(2,1)S(1)} %get-tuple-element.93), channel_id=1, source_target_pairs={{0,16},{8,24},{16,8},{24,0},{32,48},{40,56},{48,40},{56,32},{64,80... | collective-permute-start | bytes 786440 | tf_op jit(solution)/shard_map/ppermute | solution.py:402
  16.9 7.2 %collective-permute-start.6 = (bf16[32,512]{1,0:T(8,128)(2,1)S(1)}, bf16[32,512]{1,0:T(8,128)(2,1)S(1)}, u32[]{:S(2)}, u32[]{:S(2)}) collective-permute-start(bf16[32,512]{1,0:T(8,128)(2,1)S(1)} %get-tuple-element.89), channel_id=1, source_target_pairs={{0,224},{8,232},{16,240},{24,248},{32,192},{40,200},{48,208},{56,2... | collective-permute-start | bytes 98312 | tf_op jit(solution)/shard_map/ppermute | solution.py:398
  24.1 12.1 %collective-permute-start.7 = (bf16[160,512]{1,0:T(8,128)(2,1)S(1)}, bf16[160,512]{1,0:T(8,128)(2,1)S(1)}, u32[]{:S(2)}, u32[]{:S(2)}) collective-permute-start(bf16[160,512]{1,0:T(8,128)(2,1)S(1)} %get-tuple-element.99), channel_id=1, source_target_pairs={{0,32},{8,40},{16,48},{24,56},{32,0},{40,8},{48,16},{56,24},{64,96... | collective-permute-start | bytes 491528 | tf_op jit(solution)/shard_map/ppermute | solution.py:415
  25.5 5.6 %collective-permute-start.9 = (bf16[96,512]{1,0:T(8,128)(2,1)S(1)}, bf16[96,512]{1,0:T(8,128)(2,1)S(1)}, u32[]{:S(2)}, u32[]{:S(2)}) collective-permute-start(bf16[96,512]{1,0:T(8,128)(2,1)S(1)} %get-tuple-element.100), channel_id=1, source_target_pairs={{0,96},{8,104},{16,112},{24,120},{32,64},{40,72},{48,80},{56,88},{... | collective-permute-start | bytes 294920 | tf_op jit(solution)/shard_map/ppermute | solution.py:414
  27.1 9.0 %collective-permute-start.8 = (bf16[96,512]{1,0:T(8,128)(2,1)S(1)}, bf16[96,512]{1,0:T(8,128)(2,1)S(1)}, u32[]{:S(2)}, u32[]{:S(2)}) collective-permute-start(bf16[96,512]{1,0:T(8,128)(2,1)S(1)} %get-tuple-element.100), channel_id=1, source_target_pairs={{0,64},{8,72},{16,80},{24,88},{32,96},{40,104},{48,112},{56,120},{... | collective-permute-start | bytes 294920 | tf_op jit(solution)/shard_map/ppermute | solution.py:413
  37.1 11.7 %collective-permute-start.10 = (bf16[4,512,512]{2,1,0:T(8,128)(2,1)S(1)}, bf16[4,512,512]{2,1,0:T(8,128)(2,1)S(1)}, u32[]{:S(2)}, u32[]{:S(2)}) collective-permute-start(bf16[4,512,512]{2,1,0:T(8,128)(2,1)S(1)} %get-tuple-element.103), channel_id=1, source_target_pairs={{0,1},{1,0},{2,3},{3,2},{4,5},{5,4},{6,7},{7,6},{8,9},{9,8},{10,11... | collective-permute-start | bytes 6291464 | tf_op jit(solution)/shard_map/ppermute | solution.py:429
  39.1 5.9 %collective-permute-start.11 = (bf16[32,384]{1,0:T(8,128)(2,1)S(1)}, bf16[32,384]{1,0:T(8,128)(2,1)S(1)}, u32[]{:S(2)}, u32[]{:S(2)}) collective-permute-start(bf16[32,384]{1,0:T(8,128)(2,1)S(1)} %get-tuple-element.101), channel_id=1, source_target_pairs={{0,8},{8,16},{16,24},{24,0},{32,40},{40,48},{48,56},{56,32},{64,72... | collective-permute-start | bytes 73736 | tf_op jit(solution)/shard_map/ppermute | solution.py:430
  39.6 5.0 %collective-permute-start.12 = (bf16[32,384]{1,0:T(8,128)(2,1)S(1)}, bf16[32,384]{1,0:T(8,128)(2,1)S(1)}, u32[]{:S(2)}, u32[]{:S(2)}) collective-permute-start(bf16[32,384]{1,0:T(8,128)(2,1)S(1)} %get-tuple-element.106), channel_id=1, source_target_pairs={{0,16},{8,24},{16,0},{24,8},{32,48},{40,56},{48,32},{56,40},{64,80... | collective-permute-start | bytes 73736 | tf_op jit(solution)/shard_map/ppermute | solution.py:432
  41.7 3.2 %collective-permute-start.13 = (bf16[32,384]{1,0:T(8,128)(2,1)S(1)}, bf16[32,384]{1,0:T(8,128)(2,1)S(1)}, u32[]{:S(2)}, u32[]{:S(2)}) collective-permute-start(bf16[32,384]{1,0:T(8,128)(2,1)S(1)} %get-tuple-element.107), channel_id=1, source_target_pairs={{0,24},{8,0},{16,8},{24,16},{32,56},{40,32},{48,40},{56,48},{64,88... | collective-permute-start | bytes 73736 | tf_op jit(solution)/shard_map/ppermute | solution.py:431
  46.0 2.9 %collective-permute-start.14 = (bf16[512,512]{1,0:T(8,128)(2,1)S(1)}, bf16[512,512]{1,0:T(8,128)(2,1)S(1)}, u32[]{:S(2)}, u32[]{:S(2)}) collective-permute-start(bf16[512,512]{1,0:T(8,128)(2,1)S(1)} %finish.1.mine), channel_id=1, source_target_pairs={{0,1},{1,0},{2,3},{3,2},{4,5},{5,4},{6,7},{7,6},{8,9},{9,8},{10,11... | collective-permute-start | bytes 1572872 | tf_op jit(solution)/shard_map/ppermute | solution.py:455
  49.3 8.1 %collective-permute-start.16 = (bf16[256,512]{1,0:T(8,128)(2,1)S(1)}, bf16[256,512]{1,0:T(8,128)(2,1)S(1)}, u32[]{:S(2)}, u32[]{:S(2)}) collective-permute-start(bf16[256,512]{1,0:T(8,128)(2,1)S(1)} %get-tuple-element.132), channel_id=1, source_target_pairs={{0,6},{1,7},{2,0},{3,1},{4,2},{5,3},{6,4},{7,5},{8,14},{9,15},{10,... | collective-permute-start | bytes 786440 | tf_op jit(solution)/shard_map/ppermute | solution.py:482
  52.1 8.4 %collective-permute-start.15 = (bf16[256,512]{1,0:T(8,128)(2,1)S(1)}, bf16[256,512]{1,0:T(8,128)(2,1)S(1)}, u32[]{:S(2)}, u32[]{:S(2)}) collective-permute-start(bf16[256,512]{1,0:T(8,128)(2,1)S(1)} %get-tuple-element.123), channel_id=1, source_target_pairs={{0,2},{1,3},{2,4},{3,5},{4,6},{5,7},{6,0},{7,1},{8,10},{9,11},{10,... | collective-permute-start | bytes 786440 | tf_op jit(solution)/shard_map/ppermute | solution.py:481
  52.6 13.6 %collective-permute-start.19 = (bf16[256,512]{1,0:T(8,128)(2,1)S(1)}, bf16[256,512]{1,0:T(8,128)(2,1)S(1)}, u32[]{:S(2)}, u32[]{:S(2)}) collective-permute-start(bf16[256,512]{1,0:T(8,128)(2,1)S(1)} %get-tuple-element.126), channel_id=1, source_target_pairs={{0,2},{1,3},{2,4},{3,5},{4,6},{5,7},{6,0},{7,1},{8,10},{9,11},{10,... | collective-permute-start | bytes 786440 | tf_op jit(solution)/shard_map/ppermute | solution.py:494
  52.7 10.7 %collective-permute-start.18 = (bf16[256,512]{1,0:T(8,128)(2,1)S(1)}, bf16[256,512]{1,0:T(8,128)(2,1)S(1)}, u32[]{:S(2)}, u32[]{:S(2)}) collective-permute-start(bf16[256,512]{1,0:T(8,128)(2,1)S(1)} %get-tuple-element.134), channel_id=1, source_target_pairs={{0,6},{1,7},{2,0},{3,1},{4,2},{5,3},{6,4},{7,5},{8,14},{9,15},{10,... | collective-permute-start | bytes 786440 | tf_op jit(solution)/shard_map/ppermute | solution.py:495
  60.7 11.1 %collective-permute-start.17 = (bf16[256,512]{1,0:T(8,128)(2,1)S(1)}, bf16[256,512]{1,0:T(8,128)(2,1)S(1)}, u32[]{:S(2)}, u32[]{:S(2)}) collective-permute-start(bf16[256,512]{1,0:T(8,128)(2,1)S(1)} %get-tuple-element.133), channel_id=1, source_target_pairs={{0,2},{1,3},{2,4},{3,5},{4,6},{5,7},{6,0},{7,1},{8,10},{9,11},{10,... | collective-permute-start | bytes 786440 | tf_op jit(solution)/shard_map/ppermute | solution.py:510
  60.7 11.1 %collective-permute-start.20 = (bf16[256,512]{1,0:T(8,128)(2,1)S(1)}, bf16[256,512]{1,0:T(8,128)(2,1)S(1)}, u32[]{:S(2)}, u32[]{:S(2)}) collective-permute-start(bf16[256,512]{1,0:T(8,128)(2,1)S(1)} %get-tuple-element.135), channel_id=1, source_target_pairs={{0,6},{1,7},{2,0},{3,1},{4,2},{5,3},{6,4},{7,5},{8,14},{9,15},{10,... | collective-permute-start | bytes 786440 | tf_op jit(solution)/shard_map/ppermute | solution.py:511
  (5 other events, 26.9 us)
